TPU v7x, 256 devices: a whole 4x4x8 slice. The times are simulated.
256 devices in a mesh: col: 64 (over z, y_hi, x), row: 4 (over y_lo, core).
Axes of the slice: x: 4, y: 4 (y_hi: 2, y_lo: 2; y = y_hi * 2 + y_lo), z: 8, core: 2. Of those that a mesh axis runs over, the one named last changes fastest.
Arguments:
- matrix: float32 [16384, 8192], P('row', 'col'), may hold values from -40 to 40
- active: int32 [2, 32], replicated, may hold values 0 or 1
Outputs:
- rotated: float32 [16384, 8192], P('row', 'col')
All inputs are finite; a program needn't handle non-finite values.
Results may differ from a plain program's by a relative error of at most 0.00012.
Values sent between devices are 32-bit elements; how exact they have to be, the bound alone decides.
A program may use at most 64 MiB of HBM per device.

v0:
```python
import math

import jax
import jax.numpy as jnp
from jax import lax
from jax.sharding import PartitionSpec as P


def swapped(value, axis, bit):
    mask = 2**bit
    pairs = [(source, source ^ mask) for source in range(lax.axis_size(axis))]
    return lax.ppermute(value, axis, pairs)


def shifted(value, axis, steps):
    count = lax.axis_size(axis)
    pairs = [(source, (source + steps) % count) for source in range(count)]
    return lax.ppermute(value, axis, pairs)


def inverse_spd(matrix_in):
    order = matrix_in.shape[-1]
    factor = jnp.linalg.cholesky(matrix_in)
    identity = jnp.broadcast_to(jnp.eye(order, dtype=matrix_in.dtype), matrix_in.shape)
    solved = lax.linalg.triangular_solve(factor, identity, left_side=True, lower=True)
    return lax.linalg.triangular_solve(factor, solved, left_side=True, lower=True, transpose_a=True)


def rotation(gram_upper, gram_cross, gram_lower, active_flag, total_rows):
    width_block = gram_upper.shape[-1]
    scale_upper = 1.0 / jnp.sqrt(jnp.diagonal(gram_upper, axis1=-2, axis2=-1) / total_rows + 1e-06)
    scale_lower = 1.0 / jnp.sqrt(jnp.diagonal(gram_lower, axis1=-2, axis2=-1) / total_rows + 1e-06)
    coupling = (
        0.25
        / math.sqrt(total_rows * width_block)
        * scale_upper[..., :, None]
        * gram_cross
        * scale_lower[..., None, :]
    )
    coupling_t = jnp.swapaxes(coupling, -1, -2)
    outer_left = jnp.matmul(coupling, coupling_t, precision=lax.Precision.HIGHEST)
    outer_right = jnp.matmul(coupling_t, coupling, precision=lax.Precision.HIGHEST)
    identity = jnp.eye(width_block, dtype=gram_upper.dtype)
    inv_left = inverse_spd(identity + outer_left)
    inv_right = inverse_spd(identity + outer_right)
    upper_left = jnp.matmul(identity - outer_left, inv_left, precision=lax.Precision.HIGHEST)
    upper_right = 2.0 * jnp.matmul(coupling, inv_right, precision=lax.Precision.HIGHEST)
    lower_left = -2.0 * jnp.matmul(coupling_t, inv_left, precision=lax.Precision.HIGHEST)
    lower_right = jnp.matmul(identity - outer_right, inv_right, precision=lax.Precision.HIGHEST)
    rotor = jnp.concatenate(
        [
            jnp.concatenate([upper_left, upper_right], axis=-1),
            jnp.concatenate([lower_left, lower_right], axis=-1),
        ],
        axis=-2,
    )
    identity_pair = jnp.eye(2 * width_block, dtype=gram_upper.dtype)
    return jnp.where(active_flag[..., None, None] == 1, rotor, identity_pair)


def rotate_pair(upper_block, lower_block, active_row, pair_index, total_rows):
    width_block = upper_block.shape[1]
    gram_upper = jnp.einsum("ri,rj->ij", upper_block, upper_block, precision=lax.Precision.HIGHEST)
    gram_cross = jnp.einsum("ri,rj->ij", upper_block, lower_block, precision=lax.Precision.HIGHEST)
    gram_lower = jnp.einsum("ri,rj->ij", lower_block, lower_block, precision=lax.Precision.HIGHEST)
    gram_upper, gram_cross, gram_lower = lax.psum((gram_upper, gram_cross, gram_lower), "row")
    active_flag = lax.dynamic_index_in_dim(active_row, pair_index, keepdims=False)
    rotor = rotation(gram_upper, gram_cross, gram_lower, active_flag, total_rows)
    paired = jnp.concatenate([upper_block, lower_block], axis=1)
    turned = jnp.dot(paired, rotor, precision=lax.Precision.HIGHEST)
    return (turned[:, :width_block], turned[:, width_block:])


def on_device(matrix, active):
    position = lax.axis_index("col")
    pair_index = position // 2
    is_even = position % 2 == 0
    total_rows = matrix.shape[0] * lax.axis_size("row")
    section_count = active.shape[0]
    rotated = matrix
    for section_index in range(section_count):
        partner = swapped(rotated, "col", 0)
        upper_block = jnp.where(is_even, rotated, partner)
        lower_block = jnp.where(is_even, partner, rotated)
        new_upper, new_lower = rotate_pair(
            upper_block, lower_block, active[section_index], pair_index, total_rows
        )
        outgoing = jnp.where(is_even, new_upper, new_lower)
        rotated = shifted(outgoing, "col", 1)
    return rotated


def solution(mesh):
    placed = (P("row", "col"), P())
    return jax.shard_map(
        on_device, mesh=mesh, in_specs=placed, out_specs=P("row", "col"), check_vma=False
    )
```

profile of v0, /device:TPU:1, one launch (start us, length us, event | category | flops | bytes accessed | tf_op | source)
XLA Modules:
  0.0 448.4 jit_solution(3264136374222388843)
XLA Ops:
  6.5 2.0 collective-permute-start
  8.6 44.3 %collective-permute-done = f32[4096,128]{1,0:T(8,128)} collective-permute-done((f32[4096,128]{1,0:T(8,128)}, f32[4096,128]{1,0:T(8,128)}, u32[]{:S(2)}, u32[]{:S(2)}) %collective-permute-start) | collective-permute-done | bytes 2097184 | tf_op jit(solution)/shard_map/ppermute | solution.py:12
  52.9 2.5 broadcast_select_fusion.3
  55.4 4.1 fusion.81
  59.5 4.1 fusion.82
  63.6 4.1 fusion.83
  68.0 0.7 fusion.79
  68.6 46.0 %all-reduce.7.cloned.1.call-done = (f32[128,128]{1,0:T(8,128)}, f32[128,128]{1,0:T(8,128)}, f32[128,128]{1,0:T(8,128)}) async-done(((f32[128,128]{1,0:T(8,128)}, f32[128,128]{1,0:T(8,128)}, f32[128,128]{1,0:T(8,128)}), (f32[128,128]{1,0:T(8,128)}, f32[128,128]{1,0:T(8,128)}, f32[128,128]{1,0:T(8,128)})) %all-reduce.7.cloned.1.call-update) | async-done | bytes 196624 | tf_op jit(solution)/shard_map/psum | solution.py:66
  114.6 2.0 gather_fusion.1
  116.6 1.9 gather_fusion
  118.5 1.3 convert_add_fusion.2
  119.9 11.7 %cholesky.85 = f32[128,128]{1,0:T(8,128)S(1)} custom-call(f32[128,128]{1,0:T(8,128)S(1)} %fusion.51), custom_call_target="Cholesky" | custom-call | tf_op jit(solution)/shard_map/jit(cholesky)/cholesky | solution.py:23
  131.7 0.7 compare_reduce_fusion.2
  132.4 0.6 fusion.33
  133.0 9.8 %custom-call.25 = f32[1,128,128]{1,2,0:T(8,128)S(1)} custom-call(f32[1,128,128]{2,1,0:T(8,128)S(1)} %fusion.33), custom_call_target="InvertDiagBlocksLowerTriangular" | custom-call | tf_op jit(solution)/shard_map/triangular_solve/custom-call.2 | solution.py:26
  143.9 0.3 convert_add_fusion.3
  144.3 11.7 %cholesky.74 = f32[128,128]{1,0:T(8,128)S(1)} custom-call(f32[128,128]{1,0:T(8,128)S(1)} %fusion.55), custom_call_target="Cholesky" | custom-call | tf_op jit(solution)/shard_map/jit(cholesky)/cholesky | solution.py:23
  156.1 0.7 compare_reduce_fusion.3
  156.8 0.7 fusion.32
  157.5 10.2 %custom-call.23 = f32[1,128,128]{1,2,0:T(8,128)S(1)} custom-call(f32[1,128,128]{2,1,0:T(8,128)S(1)} %fusion.32), custom_call_target="InvertDiagBlocksLowerTriangular" | custom-call | tf_op jit(solution)/shard_map/triangular_solve/custom-call.2 | solution.py:26
  168.2 0.4 convolution_multiply_fusion.2
  168.6 0.3 fusion.36
  168.9 5.9 %fusion = f32[4096,256]{1,0:T(8,128)S(1)} fusion(f32[4096,128]{1,0:T(8,128)} %copy-done, f32[4096,128]{1,0:T(8,128)S(1)} %get-tuple-element.16, f32[128,128]{1,0:T(8,128)S(1)} %fusion.37, f32[128,128]{1,0:T(8,128)S(1)} %convolution_multiply_fusion.2, f32[128,128]{1,0:T(8,128)S(1)} %convolution_multiply_fusion.3, f32[128,128]{1,0:T(8,128)S(1)} %fusion.36, ...), kind=kOutput, calls=%fused_computation.4 | convolution fusion | flops 3222667264 | bytes 8650753 | tf_op jit(solution)/shard_map/dot_general | solution.py:70
  175.0 1.3 collective-permute-start.1
  176.2 51.9 %collective-permute-done.1 = f32[4096,128]{1,0:T(8,128)S(1)} collective-permute-done((f32[4096,128]{1,0:T(8,128)S(1)}, f32[4096,128]{1,0:T(8,128)S(1)}, u32[]{:S(2)}, u32[]{:S(2)}) %collective-permute-start.1) | collective-permute-done | bytes 2097184 | tf_op jit(solution)/shard_map/ppermute | solution.py:18
  228.3 46.3 %collective-permute-done.2 = f32[4096,128]{1,0:T(8,128)S(1)} collective-permute-done((f32[4096,128]{1,0:T(8,128)S(1)}, f32[4096,128]{1,0:T(8,128)S(1)}, u32[]{:S(2)}, u32[]{:S(2)}) %collective-permute-start.2) | collective-permute-done | bytes 2097184 | tf_op jit(solution)/shard_map/ppermute | solution.py:12
  274.9 4.1 fusion.84
  279.0 4.1 fusion.85
  283.1 4.1 fusion.86
  287.2 0.7 fusion.80
  287.9 38.4 %all-reduce.5.cloned.1.call-done = (f32[128,128]{1,0:T(8,128)}, f32[128,128]{1,0:T(8,128)}, f32[128,128]{1,0:T(8,128)}) async-done(((f32[128,128]{1,0:T(8,128)}, f32[128,128]{1,0:T(8,128)}, f32[128,128]{1,0:T(8,128)}), (f32[128,128]{1,0:T(8,128)}, f32[128,128]{1,0:T(8,128)}, f32[128,128]{1,0:T(8,128)})) %all-reduce.5.cloned.1.call-update) | async-done | bytes 196624 | tf_op jit(solution)/shard_map/psum | solution.py:66
  326.2 2.0 gather_fusion.3
  328.2 1.9 gather_fusion.2
  330.2 1.5 convert_add_fusion
  331.8 11.7 %cholesky.107 = f32[128,128]{1,0:T(8,128)S(1)} custom-call(f32[128,128]{1,0:T(8,128)S(1)} %fusion.43), custom_call_target="Cholesky" | custom-call | tf_op jit(solution)/shard_map/jit(cholesky)/cholesky | solution.py:23
  343.5 0.7 compare_reduce_fusion
  344.2 0.6 fusion.35
  344.8 9.8 %custom-call.29 = f32[1,128,128]{1,2,0:T(8,128)S(1)} custom-call(f32[1,128,128]{2,1,0:T(8,128)S(1)} %fusion.35), custom_call_target="InvertDiagBlocksLowerTriangular" | custom-call | tf_op jit(solution)/shard_map/triangular_solve/custom-call.2 | solution.py:26
  355.7 0.3 convert_add_fusion.1
  356.2 11.7 %cholesky.96 = f32[128,128]{1,0:T(8,128)S(1)} custom-call(f32[128,128]{1,0:T(8,128)S(1)} %fusion.47), custom_call_target="Cholesky" | custom-call | tf_op jit(solution)/shard_map/jit(cholesky)/cholesky | solution.py:23
  367.9 0.7 compare_reduce_fusion.1
  368.6 0.7 fusion.34
  369.4 10.0 %custom-call.27 = f32[1,128,128]{1,2,0:T(8,128)S(1)} custom-call(f32[1,128,128]{2,1,0:T(8,128)S(1)} %fusion.34), custom_call_target="InvertDiagBlocksLowerTriangular" | custom-call | tf_op jit(solution)/shard_map/triangular_solve/custom-call.2 | solution.py:26
  379.9 0.4 convolution_multiply_fusion
  380.5 5.9 %fusion.4 = f32[4096,256]{1,0:T(8,128)S(1)} fusion(f32[4096,128]{1,0:T(8,128)} %copy-done.1, f32[4096,128]{1,0:T(8,128)S(1)} %get-tuple-element.14, f32[128,128]{1,0:T(8,128)S(1)} %fusion.39, f32[128,128]{1,0:T(8,128)S(1)} %convolution_multiply_fusion, f32[128,128]{1,0:T(8,128)S(1)} %convolution_multiply_fusion.1, f32[128,128]{1,0:T(8,128)S(1)} %fusion.38, ...), kind=kOutput, calls=%fused_computation.8 | convolution fusion | flops 3222667264 | bytes 8650753 | tf_op jit(solution)/shard_map/dot_general | solution.py:70
  386.7 1.3 collective-permute-start.3
  387.9 51.9 %collective-permute-done.3 = f32[4096,128]{1,0:T(8,128)S(1)} collective-permute-done((f32[4096,128]{1,0:T(8,128)S(1)}, f32[4096,128]{1,0:T(8,128)S(1)}, u32[]{:S(2)}, u32[]{:S(2)}) %collective-permute-start.3) | collective-permute-done | bytes 2097184 | tf_op jit(solution)/shard_map/ppermute | solution.py:18
  439.8 1.3 copy.38
  (48 shorter events, 5.1 us)
Async XLA Ops:
  6.5 108.1 %all-reduce.7.cloned.1.call-start = ((), (), s32[]{:S(2)}) async-start(), calls=%async_computation.1 | async-start | bytes 393216 | tf_op jit(solution)/shard_map/psum | solution.py:66
  6.5 46.4 %collective-permute-start = (f32[4096,128]{1,0:T(8,128)}, f32[4096,128]{1,0:T(8,128)}, u32[]{:S(2)}, u32[]{:S(2)}) collective-permute-start(f32[4096,128]{1,0:T(8,128)} %param.7), channel_id=1, source_target_pairs={{0,4},{4,0},{8,12},{12,8},{16,20},{20,16},{24,28},{28,24},{32,36},... | collective-permute-start | bytes 6291464 | tf_op jit(solution)/shard_map/ppermute | solution.py:12
  55.4 8.2 %copy-start = (f32[4096,128]{1,0:T(8,128)}, f32[4096,128]{1,0:T(8,128)S(1)}, u32[]{:S(2)}) copy-start(f32[4096,128]{1,0:T(8,128)S(1)} %get-tuple-element.17) | copy-start | bytes 6291460
  63.6 4.4 copy-start.4
  67.7 258.6 %all-reduce.5.cloned.1.call-start = ((), (), s32[]{:S(2)}) async-start(), calls=%async_computation | async-start | bytes 393216 | tf_op jit(solution)/shard_map/psum | solution.py:66
  114.6 29.0 %copy-start.2 = (f32[128,128]{1,0:T(8,128)S(1)}, f32[128,128]{1,0:T(8,128)}, u32[]{:S(2)}) copy-start(f32[128,128]{1,0:T(8,128)} %get-tuple-element.11) | copy-start | bytes 196612
  175.0 53.2 %collective-permute-start.1 = (f32[4096,128]{1,0:T(8,128)S(1)}, f32[4096,128]{1,0:T(8,128)S(1)}, u32[]{:S(2)}, u32[]{:S(2)}) collective-permute-start(f32[4096,128]{1,0:T(8,128)S(1)} %slice_select_fusion.1), channel_id=1, source_target_pairs={{0,4},{4,8},{8,12},{12,16},{16,20},{20,24},{24,28},{28,32},{32,36}... | collective-permute-start | bytes 6291464 | tf_op jit(solution)/shard_map/ppermute | solution.py:18
  228.2 46.5 %collective-permute-start.2 = (f32[4096,128]{1,0:T(8,128)S(1)}, f32[4096,128]{1,0:T(8,128)S(1)}, u32[]{:S(2)}, u32[]{:S(2)}) collective-permute-start(f32[4096,128]{1,0:T(8,128)S(1)} %collective-permute-done.1), channel_id=1, source_target_pairs={{0,4},{4,0},{8,12},{12,8},{16,20},{20,16},{24,28},{28,24},{32,36},... | collective-permute-start | bytes 6291464 | tf_op jit(solution)/shard_map/ppermute | solution.py:12
  274.9 8.2 %copy-start.1 = (f32[4096,128]{1,0:T(8,128)}, f32[4096,128]{1,0:T(8,128)S(1)}, u32[]{:S(2)}) copy-start(f32[4096,128]{1,0:T(8,128)S(1)} %get-tuple-element.15) | copy-start | bytes 6291460
  326.2 29.2 %copy-start.3 = (f32[128,128]{1,0:T(8,128)S(1)}, f32[128,128]{1,0:T(8,128)}, u32[]{:S(2)}) copy-start(f32[128,128]{1,0:T(8,128)} %get-tuple-element.6) | copy-start | bytes 196612
  386.7 53.2 %collective-permute-start.3 = (f32[4096,128]{1,0:T(8,128)S(1)}, f32[4096,128]{1,0:T(8,128)S(1)}, u32[]{:S(2)}, u32[]{:S(2)}) collective-permute-start(f32[4096,128]{1,0:T(8,128)S(1)} %slice_select_fusion), channel_id=1, source_target_pairs={{0,4},{4,8},{8,12},{12,16},{16,20},{20,24},{24,28},{28,32},{32,36}... | collective-permute-start | bytes 6291464 | tf_op jit(solution)/shard_map/ppermute | solution.py:18
Sparse Core Ops, SparseCore 0:
  67.8 46.7 all-reduce.6
  287.3 38.8 all-reduce.4
where the time goes:
time: 457 us; the launch traced here: 448 us
  waiting for transfers between devices  279 us (61%)
  other arithmetic  96.8 us (21%)
  matrix products  44 us (10%)
  between operations  14.2 us (3%)
  local copies, waits for them, and re-layouts  9.53 us (2%)
  starting transfers between devices  4.98 us (1%)
    ppermute x2, waiting for transfers between devices, shifted(): return lax.ppermute(value, axis, pairs)  104 us
    ppermute x2, waiting for transfers between devices, swapped(): return lax.ppermute(value, axis, pairs)  90.7 us
    psum x2, waiting for transfers between devices, rotate_pair(): lax.psum((gram_upper, gram_cross, gram_lower), 'row')  84.4 us
    another operation x12, other arithmetic, inverse_spd(): factor = jnp.linalg.cholesky(matrix_in)  49.8 us
    another operation x8, other arithmetic, inverse_spd(): lax.linalg.triangular_solve(factor, solved, left_side=True, lower=True, t...  42.5 us
    dot_general x2, matrix products, rotate_pair(): turned = jnp.dot(paired, rotor, precision=lax.Precision.HIGHEST)  11.8 us
  transfers between devices with their start and end apart: 6, of which 6 were waited for; matrix products, arithmetic and copies ran while one was open for 0% of the time, Pallas kernels for 0%

commit v1 on v0

v1 whole, which is shorter than its diff:
```python
import functools
import math

import jax
import jax.numpy as jnp
from jax import lax
from jax.experimental import pallas as pl
from jax.experimental.pallas import tpu as pltpu
from jax.sharding import PartitionSpec as P

MESH = pl.DeviceIdType.MESH
CHUNK = 256
BLOCK = 4


def lane_spread(value, lane):
    return jnp.broadcast_to(value[:, lane : lane + 1], value.shape)


def eliminate(matrix_in, first):
    order = matrix_in.shape[0]
    lane = lax.broadcasted_iota(jnp.int32, (8, order), 1)
    row = lax.broadcasted_iota(jnp.int32, (8, order), 0)
    lane_all = lax.broadcasted_iota(jnp.int32, (order, order), 1)
    tiles = order // 8
    pivots = range(first, first + BLOCK)
    rows = [jnp.broadcast_to(matrix_in[p : p + 1], (8, order)) for p in pivots]
    small = [[lane_spread(rows[i], p) for p in pivots] for i in range(BLOCK)]
    columns = [lane_spread(matrix_in, p) for p in pivots]
    result = matrix_in
    for i, p in enumerate(pivots):
        inverse = 1.0 / small[i][i]
        scaled = jnp.where(lane == p, inverse, rows[i] * inverse)
        ratio = [small[i][k] * inverse for k in range(BLOCK)]
        scaled_all = jnp.concatenate([scaled] * tiles, axis=0)
        result = jnp.where(lane_all == p, 0.0, result) - columns[i] * scaled_all
        result = jnp.concatenate([jnp.where(row == p, scaled, result[:8]), result[8:]], axis=0)
        for k in range(i + 1, BLOCK):
            ratio_all = jnp.concatenate([ratio[k]] * tiles, axis=0)
            updated = columns[k] - columns[i] * ratio_all
            columns[k] = jnp.concatenate([jnp.where(row == p, ratio[k], updated[:8]), updated[8:]], axis=0)
            rows[k] = jnp.where(lane == p, 0.0, rows[k]) - small[k][i] * scaled
        for k in range(i + 1, BLOCK):
            small[k] = [small[k][j] - small[k][i] * ratio[j] if j > i else small[k][j] for j in range(BLOCK)]
    return result


def inverse_spd(matrix_in):
    order = matrix_in.shape[0]

    def body(_, value):
        for first in range(0, 8, BLOCK):
            value = eliminate(value, first)
        value = jnp.concatenate([value[8:], value[:8]], axis=0)
        return pltpu.roll(value, order - 8, 1)

    return lax.fori_loop(0, order // 8, body, matrix_in)


def split(value):
    high = value.astype(jnp.bfloat16)
    return high, (value - high.astype(jnp.float32)).astype(jnp.bfloat16)


def exact_dot(left, right, left_dim=1, right_dim=0):
    return lax.dot_general(
        left,
        right,
        (((left_dim,), (right_dim,)), ((), ())),
        precision=lax.Precision.HIGHEST,
        preferred_element_type=jnp.float32,
    )


def rotor_of(gram, flag, total_rows):
    width = gram.shape[1]
    scale_upper = 1.0 / jnp.sqrt(jnp.sum(gram[width : width + 8], axis=0, keepdims=True) / total_rows + 1e-06)
    scale_lower = 1.0 / jnp.sqrt(jnp.sum(gram[width + 8 :], axis=0, keepdims=True) / total_rows + 1e-06)
    scale_rows = jnp.broadcast_to(scale_upper, (width, width)).T
    coupling = 0.25 / math.sqrt(total_rows * width) * flag * scale_rows * gram[:width] * scale_lower
    row = lax.broadcasted_iota(jnp.int32, (width, width), 0)
    lane = lax.broadcasted_iota(jnp.int32, (width, width), 1)
    identity = jnp.where(row == lane, 1.0, 0.0)
    inv_left = inverse_spd(identity + exact_dot(coupling, coupling, 1, 1))
    product = exact_dot(inv_left, coupling)
    lower_right = identity - 2.0 * exact_dot(coupling, product, 0, 0)
    top = jnp.concatenate([2.0 * inv_left - identity, 2.0 * product], axis=1)
    bottom = jnp.concatenate([-2.0 * product.T, lower_right], axis=1)
    return jnp.concatenate([top, bottom], axis=0)


def kernel(
    total_rows, col_count, matrix_ref, active_ref, out_ref,
    first, second, sending, result, gram, norms, shared, arrived, rotor_parts,
    own_sem, a_send, a_recv, b_send, b_recv, g_send, g_recv, c_send, c_recv, local_sem,
):
    col, row = lax.axis_index("col"), lax.axis_index("row")
    odd = lax.rem(col, 2)
    pair = col // 2
    parity = lax.rem(pair, 2)
    half = lax.rem(odd + parity, 2)
    width = matrix_ref.shape[1]
    half_rows = matrix_ref.shape[0] // 2
    chunks = half_rows // CHUNK
    upper_col = 2 * pair

    def wrapped(position):
        return lax.rem(position + col_count, col_count)

    partner = (col + 1 - 2 * odd, row)
    sibling = (col, row + 1 - 2 * lax.rem(row, 2))
    beside = (col, lax.rem(row + 2, 4))
    b_target = (wrapped(upper_col + 3 - odd), row)
    b_source = (wrapped(upper_col - 1 - odd), row)
    next_upper = (wrapped(upper_col + 2), row)
    last_upper = (wrapped(upper_col - 2), row)

    barrier = pltpu.get_barrier_semaphore()
    for device in (partner, sibling, beside, b_target, b_source):
        pl.semaphore_signal(barrier, inc=1, device_id=device, device_id_type=MESH)

    @pl.when(odd == 0)
    def _():
        for device in (next_upper, last_upper):
            pl.semaphore_signal(barrier, inc=1, device_id=device, device_id_type=MESH)

    pl.semaphore_wait(barrier, 7 - 2 * odd)

    def rows_of(which, chunk):
        return pl.ds(pl.multiple_of(which * half_rows + chunk * CHUNK, CHUNK), CHUNK)

    def a_copy(chunk):
        return pltpu.make_async_remote_copy(
            src_ref=matrix_ref.at[rows_of(1 - half, chunk)],
            dst_ref=first.at[odd, rows_of(0, chunk)],
            send_sem=a_send.at[chunk],
            recv_sem=a_recv.at[chunk],
            device_id=partner,
            device_id_type=MESH,
        )

    def b_copy(chunk):
        return pltpu.make_async_remote_copy(
            src_ref=sending.at[rows_of(0, chunk)],
            dst_ref=second.at[0, rows_of(0, chunk)],
            send_sem=b_send.at[chunk],
            recv_sem=b_recv.at[chunk],
            device_id=b_target,
            device_id_type=MESH,
        )

    def c_copy(side, chunk, origin, device):
        return pltpu.make_async_remote_copy(
            src_ref=result.at[side, rows_of(0, chunk)],
            dst_ref=out_ref.at[rows_of(half, chunk)],
            send_sem=c_send.at[side, chunk],
            recv_sem=c_recv.at[origin, chunk],
            device_id=device,
            device_id_type=MESH,
        )

    def c_upper(chunk):
        return c_copy(0, chunk, 0, partner)

    def c_lower(chunk):
        return c_copy(1, chunk, odd, next_upper)

    def c_local(chunk):
        return pltpu.make_async_copy(
            result.at[0, rows_of(0, chunk)], out_ref.at[rows_of(half, chunk)], local_sem.at[chunk]
        )

    def each_chunk(body):
        lax.fori_loop(0, chunks, lambda chunk, carry: (body(chunk), carry)[1], 0)

    own = pltpu.make_async_copy(
        matrix_ref.at[pl.ds(pl.multiple_of(half * half_rows, CHUNK), half_rows)], first.at[odd], own_sem
    )
    each_chunk(lambda chunk: a_copy(chunk).start())
    own.start()

    def clear():
        gram[...] = jnp.zeros_like(gram)
        norms[...] = jnp.zeros_like(norms)

    def add_gram(held, chunk):
        upper = held[0, rows_of(0, chunk)]
        lower = held[1, rows_of(0, chunk)]
        gram[...] += lax.dot_general(
            jnp.concatenate(split(upper), axis=1),
            jnp.concatenate(split(lower), axis=1),
            (((0,), (0,)), ((), ())),
            preferred_element_type=jnp.float32,
        )
        norms[0] += jnp.sum((upper * upper).reshape(CHUNK // 8, 8, width), axis=0)
        norms[1] += jnp.sum((lower * lower).reshape(CHUNK // 8, 8, width), axis=0)

    def make_rotor(step):
        shared[step, 0, :width] = (gram[:width, :width] + gram[width:, width:]) + (
            gram[:width, width:] + gram[width:, :width]
        )
        shared[step, 0, width : width + 8] = norms[0]
        shared[step, 0, width + 8 :] = norms[1]
        for stage, device in enumerate((sibling, beside, partner)):
            copy = pltpu.make_async_remote_copy(
                src_ref=shared.at[step, stage],
                dst_ref=arrived.at[step, stage],
                send_sem=g_send.at[step, stage],
                recv_sem=g_recv.at[step, stage],
                device_id=device,
                device_id_type=MESH,
            )
            copy.start()
            copy.wait()
            shared[step, stage + 1] = shared[step, stage] + arrived[step, stage]
        flag = active_ref[step, pair].astype(jnp.float32)
        high, low = split(rotor_of(shared[step, 3], flag, total_rows))
        rotor_parts[: 2 * width] = high
        rotor_parts[2 * width : 4 * width] = high
        rotor_parts[4 * width :] = low

    def turned(held, chunk):
        paired = jnp.concatenate([held[0, rows_of(0, chunk)], held[1, rows_of(0, chunk)]], axis=1)
        high, low = split(paired)
        return jnp.dot(
            jnp.concatenate([high, low, high], axis=1), rotor_parts[...], preferred_element_type=jnp.float32
        )

    clear()
    own.wait()

    def gather_first(chunk):
        a_copy(chunk).wait_recv()
        add_gram(first, chunk)

    each_chunk(gather_first)
    make_rotor(0)

    def turn_first(chunk):
        value = turned(first, chunk)
        sending[rows_of(0, chunk)] = value[:, width:]
        b_copy(chunk).start()
        second[1, rows_of(0, chunk)] = value[:, :width]

    each_chunk(turn_first)
    clear()

    def gather_second(chunk):
        b_copy(chunk).wait_recv()
        add_gram(second, chunk)

    each_chunk(gather_second)
    make_rotor(1)

    def turn_second(chunk):
        value = turned(second, chunk)
        result[1, rows_of(0, chunk)] = value[:, width:]
        c_lower(chunk).start()
        result[0, rows_of(0, chunk)] = value[:, :width]

        @pl.when(odd == 0)
        def _():
            c_upper(chunk).start()

        @pl.when(odd == 1)
        def _():
            c_local(chunk).start()

    each_chunk(turn_second)

    def finish(chunk):
        a_copy(chunk).wait_send()
        b_copy(chunk).wait_send()
        c_lower(chunk).wait_send()
        c_copy(0, chunk, 0, partner).wait_recv()

        @pl.when(odd == 0)
        def _():
            c_upper(chunk).wait_send()
            c_copy(0, chunk, 1, partner).wait_recv()

        @pl.when(odd == 1)
        def _():
            c_local(chunk).wait()

    each_chunk(finish)


def solution(mesh):
    col_count = mesh.shape["col"]

    def on_device(matrix, active):
        rows, width = matrix.shape
        half_rows = rows // 2
        chunks = half_rows // CHUNK
        total_rows = rows * mesh.shape["row"]
        payload = width + 16
        dma = pltpu.SemaphoreType.DMA
        return pl.pallas_call(
            functools.partial(kernel, total_rows, col_count),
            out_shape=jax.ShapeDtypeStruct(matrix.shape, jnp.float32),
            in_specs=[pl.BlockSpec(memory_space=pl.ANY), pl.BlockSpec(memory_space=pltpu.SMEM)],
            out_specs=pl.BlockSpec(memory_space=pl.ANY),
            scratch_shapes=[
                pltpu.VMEM((2, half_rows, width), jnp.float32),
                pltpu.VMEM((2, half_rows, width), jnp.float32),
                pltpu.VMEM((half_rows, width), jnp.float32),
                pltpu.VMEM((2, half_rows, width), jnp.float32),
                pltpu.VMEM((2 * width, 2 * width), jnp.float32),
                pltpu.VMEM((2, 8, width), jnp.float32),
                pltpu.VMEM((2, 4, payload, width), jnp.float32),
                pltpu.VMEM((2, 3, payload, width), jnp.float32),
                pltpu.VMEM((6 * width, 2 * width), jnp.bfloat16),
                dma(()),
                dma((chunks,)),
                dma((chunks,)),
                dma((chunks,)),
                dma((chunks,)),
                dma((2, 3)),
                dma((2, 3)),
                dma((2, chunks)),
                dma((2, chunks)),
                dma((chunks,)),
            ],
            compiler_params=pltpu.CompilerParams(
                collective_id=0, has_side_effects=True, vmem_limit_bytes=40 * 2**20
            ),
            name="tournament",
        )(matrix, active)

    return jax.shard_map(
        on_device, mesh=mesh, in_specs=(P("row", "col"), P()), out_specs=P("row", "col"), check_vma=False
    )
```

time: 457 us -> 141 us (0.31); the launches traced: 448 us -> 140 us
  waiting for transfers between devices: 279 us -> 0 us
  Pallas kernels: 0 us -> 137 us
  other arithmetic: 96.8 us -> 0 us
  matrix products: 44 us -> 0 us
  between operations: 14.2 us -> 0.01 us
  local copies, waits for them, and re-layouts: 9.53 us -> 3.59 us
  starting transfers between devices: 4.98 us -> 0 us
    ppermute x4 -> x0, waiting for transfers between devices: 194 us -> none  [the longest x2 104 us: shifted(): return lax.ppermute(value, axis, pairs)]
    pallas_call x0 -> x1, Pallas kernels: none -> 137 us  [on_device(): pl.pallas_call(functools.partial(kernel, total_rows, col_count), out_shap...]
    another operation x20 -> x0, other arithmetic: 92.2 us -> none  [the longest x12 49.8 us: inverse_spd(): factor = jnp.linalg.cholesky(matrix_in)]
    psum x2 -> x0, waiting for transfers between devices: 84.4 us -> none  [rotate_pair(): lax.psum((gram_upper, gram_cross, gram_lower), 'row')]
    dot_general x20 -> x0, matrix products: 42 us -> none  [the longest x2 11.8 us: rotate_pair(): turned = jnp.dot(paired, rotor, precision=lax.Precision.HIGHEST)]
    gather x4 -> x0, local copies, waits for them, and re-layouts: 7.82 us -> none  [the longest x2 3.94 us: rotation(): jnp.diagonal(gram_lower, axis1=-2, axis2=-1) / total_rows + 1e-06]
    ppermute x4 -> x0, starting transfers between devices: 4.73 us -> none  [the longest x2 2.53 us: shifted(): return lax.ppermute(value, axis, pairs)]
  transfers between devices with their start and end apart: 6 -> 0, of which waited for: 6 -> 0; matrix products, arithmetic and copies ran while one was open for 0% -> 0% of each run, Pallas kernels for 0% -> 0%
where the time goes in v1:
time: 141 us; the launch traced here: 140 us
  Pallas kernels  137 us (97%)
  local copies, waits for them, and re-layouts  3.59 us (3%)
    pallas_call x1, Pallas kernels, on_device(): pl.pallas_call(functools.partial(kernel, total_rows, col_count), out_shap...  137 us
    unnamed x5, local copies, waits for them, and re-layouts  3.59 us

profile of v1, /device:TPU:1, one launch (start us, length us, event | category | flops | bytes accessed | tf_op | source)
XLA Modules:
  0.0 140.3 jit_solution(5601455354180550959)
XLA Ops:
  0.0 0.0 copy-start
  0.0 1.6 %copy-done = f32[4096,128]{1,0:T(8,128)S(1)} copy-done((f32[4096,128]{1,0:T(8,128)S(1)}, f32[4096,128]{1,0:T(8,128)}, u32[]{:S(2)}) %copy-start) | copy-done | bytes 2097176
  1.6 0.0 copy-start.1
  1.6 0.7 copy-done.1
  2.3 136.7 %tournament.1 = f32[4096,128]{1,0:T(8,128)S(1)} custom-call(f32[4096,128]{1,0:T(8,128)S(1)} %copy-done, s32[2,32]{1,0:T(2,128)S(1)} %copy-done.1), custom_call_target="tpu_custom_call" | custom-call | tf_op jit(solution)/shard_map/tournament/pallas_call | solution.py:299
  139.0 1.3 copy.4
Async XLA Ops:
  0.0 1.6 %copy-start = (f32[4096,128]{1,0:T(8,128)S(1)}, f32[4096,128]{1,0:T(8,128)}, u32[]{:S(2)}) copy-start(f32[4096,128]{1,0:T(8,128)} %matrix_ref.1) | copy-start | bytes 6291460
  1.6 0.7 copy-start.1

commit v2 on v1

--- a/solution.py
+++ b/solution.py
@@ -91,7 +91,7 @@
 
 def kernel(
     total_rows, col_count, matrix_ref, active_ref, out_ref,
-    first, second, sending, result, gram, norms, shared, arrived, rotor_parts,
+    first, second, sending, result, relay, gram, norms, shared, arrived, rotor_parts,
     own_sem, a_send, a_recv, b_send, b_recv, g_send, g_recv, c_send, c_recv, local_sem,
 ):
     col, row = lax.axis_index("col"), lax.axis_index("row")
@@ -112,19 +112,11 @@
     beside = (col, lax.rem(row + 2, 4))
     b_target = (wrapped(upper_col + 3 - odd), row)
     b_source = (wrapped(upper_col - 1 - odd), row)
-    next_upper = (wrapped(upper_col + 2), row)
-    last_upper = (wrapped(upper_col - 2), row)
 
     barrier = pltpu.get_barrier_semaphore()
     for device in (partner, sibling, beside, b_target, b_source):
         pl.semaphore_signal(barrier, inc=1, device_id=device, device_id_type=MESH)
-
-    @pl.when(odd == 0)
-    def _():
-        for device in (next_upper, last_upper):
-            pl.semaphore_signal(barrier, inc=1, device_id=device, device_id_type=MESH)
-
-    pl.semaphore_wait(barrier, 7 - 2 * odd)
+    pl.semaphore_wait(barrier, 5)
 
     def rows_of(which, chunk):
         return pl.ds(pl.multiple_of(which * half_rows + chunk * CHUNK, CHUNK), CHUNK)
@@ -149,21 +141,34 @@
             device_id_type=MESH,
         )
 
-    def c_copy(side, chunk, origin, device):
+    def to_output(source, send, recv, chunk, device):
         return pltpu.make_async_remote_copy(
-            src_ref=result.at[side, rows_of(0, chunk)],
+            src_ref=source.at[rows_of(0, chunk)],
             dst_ref=out_ref.at[rows_of(half, chunk)],
-            send_sem=c_send.at[side, chunk],
-            recv_sem=c_recv.at[origin, chunk],
+            send_sem=send.at[chunk],
+            recv_sem=recv.at[chunk],
             device_id=device,
             device_id_type=MESH,
         )
 
     def c_upper(chunk):
-        return c_copy(0, chunk, 0, partner)
+        return to_output(result.at[0], c_send.at[0], c_recv.at[0], chunk, partner)
 
     def c_lower(chunk):
-        return c_copy(1, chunk, odd, next_upper)
+        return to_output(result.at[1], c_send.at[1], c_recv.at[1], chunk, b_target)
+
+    def c_passed(chunk):
+        return to_output(relay, c_send.at[0], c_recv.at[0], chunk, partner)
+
+    def c_relay(chunk):
+        return pltpu.make_async_remote_copy(
+            src_ref=result.at[1, rows_of(0, chunk)],
+            dst_ref=relay.at[rows_of(0, chunk)],
+            send_sem=c_send.at[1, chunk],
+            recv_sem=c_recv.at[1, chunk],
+            device_id=b_target,
+            device_id_type=MESH,
+        )
 
     def c_local(chunk):
         return pltpu.make_async_copy(
@@ -255,29 +260,38 @@
     def turn_second(chunk):
         value = turned(second, chunk)
         result[1, rows_of(0, chunk)] = value[:, width:]
-        c_lower(chunk).start()
         result[0, rows_of(0, chunk)] = value[:, :width]
 
         @pl.when(odd == 0)
         def _():
+            c_relay(chunk).start()
             c_upper(chunk).start()
 
         @pl.when(odd == 1)
         def _():
+            c_lower(chunk).start()
             c_local(chunk).start()
 
     each_chunk(turn_second)
+
+    @pl.when(odd == 1)
+    def _():
+        def pass_on(chunk):
+            c_relay(chunk).wait_recv()
+            c_passed(chunk).start()
+
+        each_chunk(pass_on)
 
     def finish(chunk):
         a_copy(chunk).wait_send()
         b_copy(chunk).wait_send()
         c_lower(chunk).wait_send()
-        c_copy(0, chunk, 0, partner).wait_recv()
+        c_upper(chunk).wait_send()
+        c_upper(chunk).wait_recv()
 
         @pl.when(odd == 0)
         def _():
-            c_upper(chunk).wait_send()
-            c_copy(0, chunk, 1, partner).wait_recv()
+            c_lower(chunk).wait_recv()
 
         @pl.when(odd == 1)
         def _():
@@ -306,6 +320,7 @@
                 pltpu.VMEM((2, half_rows, width), jnp.float32),
                 pltpu.VMEM((half_rows, width), jnp.float32),
                 pltpu.VMEM((2, half_rows, width), jnp.float32),
+                pltpu.VMEM((half_rows, width), jnp.float32),
                 pltpu.VMEM((2 * width, 2 * width), jnp.float32),
                 pltpu.VMEM((2, 8, width), jnp.float32),
                 pltpu.VMEM((2, 4, payload, width), jnp.float32),

time: 141 us -> 123 us (0.87)
  Pallas kernels: 137 us -> 119 us
    pallas_call x1, Pallas kernels: 137 us -> 119 us  [on_device(): pl.pallas_call(functools.partial(kernel, total_rows, col_count), out_shap...]
where the time goes in v2:
time: 123 us; the launch traced here: 122 us
  Pallas kernels  119 us (97%)
  local copies, waits for them, and re-layouts  3.59 us (3%)
    pallas_call x1, Pallas kernels, on_device(): pl.pallas_call(functools.partial(kernel, total_rows, col_count), out_shap...  119 us
    unnamed x5, local copies, waits for them, and re-layouts  3.59 us

profile of v2, /device:TPU:1, one launch (start us, length us, event | category | flops | bytes accessed | tf_op | source)
XLA Modules:
  0.0 122.2 jit_solution(3699475051342043239)
XLA Ops:
  0.0 0.0 copy-start
  0.0 1.6 %copy-done = f32[4096,128]{1,0:T(8,128)S(1)} copy-done((f32[4096,128]{1,0:T(8,128)S(1)}, f32[4096,128]{1,0:T(8,128)}, u32[]{:S(2)}) %copy-start) | copy-done | bytes 2097176
  1.6 0.0 copy-start.1
  1.6 0.7 copy-done.1
  2.3 118.6 %tournament.1 = f32[4096,128]{1,0:T(8,128)S(1)} custom-call(f32[4096,128]{1,0:T(8,128)S(1)} %copy-done, s32[2,32]{1,0:T(2,128)S(1)} %copy-done.1), custom_call_target="tpu_custom_call" | custom-call | tf_op jit(solution)/shard_map/tournament/pallas_call | solution.py:313
  120.9 1.3 %copy.4 = f32[4096,128]{1,0:T(8,128)} copy(f32[4096,128]{1,0:T(8,128)S(1)} %tournament.1) | data formatting | bytes 4194304
Async XLA Ops:
  0.0 1.6 %copy-start = (f32[4096,128]{1,0:T(8,128)S(1)}, f32[4096,128]{1,0:T(8,128)}, u32[]{:S(2)}) copy-start(f32[4096,128]{1,0:T(8,128)} %matrix_ref.1) | copy-start | bytes 6291460
  1.6 0.7 copy-start.1

commit v3 on v2

--- a/solution.py
+++ b/solution.py
@@ -10,51 +10,58 @@
 
 MESH = pl.DeviceIdType.MESH
 CHUNK = 256
-BLOCK = 4
+TILE = 8
 
 
 def lane_spread(value, lane):
     return jnp.broadcast_to(value[:, lane : lane + 1], value.shape)
 
 
-def eliminate(matrix_in, first):
-    order = matrix_in.shape[0]
-    lane = lax.broadcasted_iota(jnp.int32, (8, order), 1)
-    row = lax.broadcasted_iota(jnp.int32, (8, order), 0)
-    lane_all = lax.broadcasted_iota(jnp.int32, (order, order), 1)
-    tiles = order // 8
-    pivots = range(first, first + BLOCK)
-    rows = [jnp.broadcast_to(matrix_in[p : p + 1], (8, order)) for p in pivots]
-    small = [[lane_spread(rows[i], p) for p in pivots] for i in range(BLOCK)]
-    columns = [lane_spread(matrix_in, p) for p in pivots]
-    result = matrix_in
-    for i, p in enumerate(pivots):
-        inverse = 1.0 / small[i][i]
-        scaled = jnp.where(lane == p, inverse, rows[i] * inverse)
-        ratio = [small[i][k] * inverse for k in range(BLOCK)]
-        scaled_all = jnp.concatenate([scaled] * tiles, axis=0)
-        result = jnp.where(lane_all == p, 0.0, result) - columns[i] * scaled_all
-        result = jnp.concatenate([jnp.where(row == p, scaled, result[:8]), result[8:]], axis=0)
-        for k in range(i + 1, BLOCK):
-            ratio_all = jnp.concatenate([ratio[k]] * tiles, axis=0)
-            updated = columns[k] - columns[i] * ratio_all
-            columns[k] = jnp.concatenate([jnp.where(row == p, ratio[k], updated[:8]), updated[8:]], axis=0)
-            rows[k] = jnp.where(lane == p, 0.0, rows[k]) - small[k][i] * scaled
-        for k in range(i + 1, BLOCK):
-            small[k] = [small[k][j] - small[k][i] * ratio[j] if j > i else small[k][j] for j in range(BLOCK)]
+def eliminate(tiles, block):
+    size = TILE
+    first = size * block
+    shape = tiles[0].shape
+    lane = lax.broadcasted_iota(jnp.int32, shape, 1)
+    row = lax.broadcasted_iota(jnp.int32, shape, 0)
+    inside = (lane >= first) & (lane < first + size)
+    rows = [jnp.broadcast_to(tiles[block][i : i + 1], shape) for i in range(size)]
+    small = {(i, j): lane_spread(rows[i], first + j) for i in range(size) for j in range(i, size)}
+    rows = [jnp.where(inside, jnp.where(lane == first + i, 1.0, 0.0), rows[i]) for i in range(size)]
+    inverse, ratio = [None] * size, {}
+    for i in range(size):
+        if i % 2 == 0:
+            head, side, tail = small[i, i], small[i, i + 1], small[i + 1, i + 1]
+            inverse[i] = 1.0 / head
+            inverse[i + 1] = head * (1.0 / (head * tail - side * side))
+        for k in range(i + 1, size):
+            ratio[i, k] = small[i, k] * inverse[i]
+            for j in range(k, size):
+                small[k, j] = small[k, j] - ratio[i, k] * small[i, j]
+            rows[k] = rows[k] - ratio[i, k] * rows[i]
+    for i in reversed(range(size)):
+        rows[i] = rows[i] * inverse[i]
+        for k in range(i + 1, size):
+            rows[i] = rows[i] - ratio[i, k] * rows[k]
+    result = list(tiles)
+    for other in range(len(tiles)):
+        if other != block:
+            value = jnp.where(inside, 0.0, tiles[other])
+            for i in range(size):
+                value = value - lane_spread(tiles[other], first + i) * rows[i]
+            result[other] = value
+    solved = rows[0]
+    for i in range(1, size):
+        solved = jnp.where(row == i, rows[i], solved)
+    result[block] = solved
     return result
 
 
 def inverse_spd(matrix_in):
     order = matrix_in.shape[0]
-
-    def body(_, value):
-        for first in range(0, 8, BLOCK):
-            value = eliminate(value, first)
-        value = jnp.concatenate([value[8:], value[:8]], axis=0)
-        return pltpu.roll(value, order - 8, 1)
-
-    return lax.fori_loop(0, order // 8, body, matrix_in)
+    tiles = [matrix_in[i : i + TILE] for i in range(0, order, TILE)]
+    for block in range(order // TILE):
+        tiles = eliminate(tiles, block)
+    return jnp.concatenate(tiles, axis=0)
 
 
 def split(value):
@@ -72,12 +79,12 @@
     )
 
 
-def rotor_of(gram, flag, total_rows):
-    width = gram.shape[1]
-    scale_upper = 1.0 / jnp.sqrt(jnp.sum(gram[width : width + 8], axis=0, keepdims=True) / total_rows + 1e-06)
-    scale_lower = 1.0 / jnp.sqrt(jnp.sum(gram[width + 8 :], axis=0, keepdims=True) / total_rows + 1e-06)
+def rotor_of(cross, norm_upper, norm_lower, flag, total_rows):
+    width = cross.shape[1]
+    scale_upper = 1.0 / jnp.sqrt(jnp.sum(norm_upper, axis=0, keepdims=True) / total_rows + 1e-06)
+    scale_lower = 1.0 / jnp.sqrt(jnp.sum(norm_lower, axis=0, keepdims=True) / total_rows + 1e-06)
     scale_rows = jnp.broadcast_to(scale_upper, (width, width)).T
-    coupling = 0.25 / math.sqrt(total_rows * width) * flag * scale_rows * gram[:width] * scale_lower
+    coupling = 0.25 / math.sqrt(total_rows * width) * flag * scale_rows * cross * scale_lower
     row = lax.broadcasted_iota(jnp.int32, (width, width), 0)
     lane = lax.broadcasted_iota(jnp.int32, (width, width), 1)
     identity = jnp.where(row == lane, 1.0, 0.0)
@@ -91,11 +98,11 @@
 
 def kernel(
     total_rows, col_count, matrix_ref, active_ref, out_ref,
-    first, second, sending, result, relay, gram, norms, shared, arrived, rotor_parts,
-    own_sem, a_send, a_recv, b_send, b_recv, g_send, g_recv, c_send, c_recv, local_sem,
+    first, second, sending, result, relay, gram, norms, partial, arrived, summed, shared, rotor_parts, flags,
+    flag_sem, own_sem, a_send, a_recv, b_send, b_recv, g_send, g_recv, c_send, c_recv, local_sem,
 ):
     col, row = lax.axis_index("col"), lax.axis_index("row")
-    odd = lax.rem(col, 2)
+    odd, core = lax.rem(col, 2), lax.rem(row, 2)
     pair = col // 2
     parity = lax.rem(pair, 2)
     half = lax.rem(odd + parity, 2)
@@ -110,13 +117,14 @@
     partner = (col + 1 - 2 * odd, row)
     sibling = (col, row + 1 - 2 * lax.rem(row, 2))
     beside = (col, lax.rem(row + 2, 4))
+    across = (col + 1 - 2 * odd, lax.rem(row + 2, 4))
     b_target = (wrapped(upper_col + 3 - odd), row)
     b_source = (wrapped(upper_col - 1 - odd), row)
 
     barrier = pltpu.get_barrier_semaphore()
-    for device in (partner, sibling, beside, b_target, b_source):
+    for device in (partner, sibling, beside, across, b_target, b_source):
         pl.semaphore_signal(barrier, inc=1, device_id=device, device_id_type=MESH)
-    pl.semaphore_wait(barrier, 5)
+    pl.semaphore_wait(barrier, 6)
 
     def rows_of(which, chunk):
         return pl.ds(pl.multiple_of(which * half_rows + chunk * CHUNK, CHUNK), CHUNK)
@@ -175,6 +183,16 @@
             result.at[0, rows_of(0, chunk)], out_ref.at[rows_of(half, chunk)], local_sem.at[chunk]
         )
 
+    def g_copy(source, target, step, stage, device):
+        return pltpu.make_async_remote_copy(
+            src_ref=source,
+            dst_ref=target,
+            send_sem=g_send.at[step, stage],
+            recv_sem=g_recv.at[step, stage],
+            device_id=device,
+            device_id_type=MESH,
+        )
+
     def each_chunk(body):
         lax.fori_loop(0, chunks, lambda chunk, carry: (body(chunk), carry)[1], 0)
 
@@ -183,6 +201,8 @@
     )
     each_chunk(lambda chunk: a_copy(chunk).start())
     own.start()
+    flag_copy = pltpu.make_async_copy(active_ref, flags, flag_sem)
+    flag_copy.start()
 
     def clear():
         gram[...] = jnp.zeros_like(gram)
@@ -201,25 +221,31 @@
         norms[1] += jnp.sum((lower * lower).reshape(CHUNK // 8, 8, width), axis=0)
 
     def make_rotor(step):
-        shared[step, 0, :width] = (gram[:width, :width] + gram[width:, width:]) + (
-            gram[:width, width:] + gram[width:, :width]
-        )
-        shared[step, 0, width : width + 8] = norms[0]
-        shared[step, 0, width + 8 :] = norms[1]
-        for stage, device in enumerate((sibling, beside, partner)):
-            copy = pltpu.make_async_remote_copy(
-                src_ref=shared.at[step, stage],
-                dst_ref=arrived.at[step, stage],
-                send_sem=g_send.at[step, stage],
-                recv_sem=g_recv.at[step, stage],
-                device_id=device,
-                device_id_type=MESH,
-            )
+        middle = width // 2
+        cross = (gram[:width, :width] + gram[width:, width:]) + (gram[:width, width:] + gram[width:, :width])
+        for part in range(2):
+            partial[step, part, :middle] = cross[part * middle : (part + 1) * middle]
+            partial[step, part, middle:] = norms[part]
+        copy = g_copy(partial.at[step, 1 - core], arrived.at[step, 0], step, 0, sibling)
+        copy.start()
+        copy.wait()
+        summed[step] = partial[step, core] + arrived[step, 0]
+        copies = [
+            g_copy(summed.at[step], arrived.at[step, stage], step, stage, device)
+            for stage, device in ((1, partner), (2, beside), (3, across))
+        ]
+        for copy in copies:
             copy.start()
+        for copy in copies:
             copy.wait()
-            shared[step, stage + 1] = shared[step, stage] + arrived[step, stage]
-        flag = active_ref[step, pair].astype(jnp.float32)
-        high, low = split(rotor_of(shared[step, 3], flag, total_rows))
+        shared[step, core] = (summed[step] + arrived[step, 1]) + (arrived[step, 2] + arrived[step, 3])
+        copy = g_copy(shared.at[step, core], shared.at[step, core], step, 4, sibling)
+        copy.start()
+        copy.wait()
+        flag = flags[step, pair].astype(jnp.float32)
+        cross = jnp.concatenate([shared[step, 0, :middle], shared[step, 1, :middle]], axis=0)
+        rotor = rotor_of(cross, shared[step, 0, middle:], shared[step, 1, middle:], flag, total_rows)
+        high, low = split(rotor)
         rotor_parts[: 2 * width] = high
         rotor_parts[2 * width : 4 * width] = high
         rotor_parts[4 * width :] = low
@@ -233,6 +259,7 @@
 
     clear()
     own.wait()
+    flag_copy.wait()
 
     def gather_first(chunk):
         a_copy(chunk).wait_recv()
@@ -308,12 +335,12 @@
         half_rows = rows // 2
         chunks = half_rows // CHUNK
         total_rows = rows * mesh.shape["row"]
-        payload = width + 16
+        payload = width // 2 + TILE
         dma = pltpu.SemaphoreType.DMA
         return pl.pallas_call(
             functools.partial(kernel, total_rows, col_count),
             out_shape=jax.ShapeDtypeStruct(matrix.shape, jnp.float32),
-            in_specs=[pl.BlockSpec(memory_space=pl.ANY), pl.BlockSpec(memory_space=pltpu.SMEM)],
+            in_specs=[pl.BlockSpec(memory_space=pl.ANY)] * 2,
             out_specs=pl.BlockSpec(memory_space=pl.ANY),
             scratch_shapes=[
                 pltpu.VMEM((2, half_rows, width), jnp.float32),
@@ -323,22 +350,26 @@
                 pltpu.VMEM((half_rows, width), jnp.float32),
                 pltpu.VMEM((2 * width, 2 * width), jnp.float32),
                 pltpu.VMEM((2, 8, width), jnp.float32),
+                pltpu.VMEM((2, 2, payload, width), jnp.float32),
                 pltpu.VMEM((2, 4, payload, width), jnp.float32),
-                pltpu.VMEM((2, 3, payload, width), jnp.float32),
+                pltpu.VMEM((2, payload, width), jnp.float32),
+                pltpu.VMEM((2, 2, payload, width), jnp.float32),
                 pltpu.VMEM((6 * width, 2 * width), jnp.bfloat16),
+                pltpu.SMEM(active.shape, jnp.int32),
                 dma(()),
-                dma((chunks,)),
-                dma((chunks,)),
-                dma((chunks,)),
-                dma((chunks,)),
-                dma((2, 3)),
-                dma((2, 3)),
+                dma(()),
+                dma((chunks,)),
+                dma((chunks,)),
+                dma((chunks,)),
+                dma((chunks,)),
+                dma((2, 5)),
+                dma((2, 5)),
                 dma((2, chunks)),
                 dma((2, chunks)),
                 dma((chunks,)),
             ],
             compiler_params=pltpu.CompilerParams(
-                collective_id=0, has_side_effects=True, vmem_limit_bytes=40 * 2**20
+                collective_id=0, has_side_effects=True, vmem_limit_bytes=50 * 2**20
             ),
             name="tournament",
         )(matrix, active)

time: 123 us -> 116 us (0.943)
  Pallas kernels: 119 us -> 114 us
  local copies, waits for them, and re-layouts: 3.59 us -> 2 us
    pallas_call x1, Pallas kernels: 119 us -> 114 us  [on_device(): pl.pallas_call(functools.partial(kernel, total_rows, col_count), out_shap...]
    unnamed x5 -> x3, local copies, waits for them, and re-layouts: 3.59 us -> 2 us
where the time goes in v3:
time: 116 us
  Pallas kernels  114 us (98%)
  local copies, waits for them, and re-layouts  2 us (2%)
    pallas_call x1, Pallas kernels, on_device(): pl.pallas_call(functools.partial(kernel, total_rows, col_count), out_shap...  114 us

profile of v3, /device:TPU:1, one launch (start us, length us, event | category | flops | bytes accessed | tf_op | source)
XLA Modules:
  0.0 116.2 jit_solution(4782222073646606188)
XLA Ops:
  0.0 0.0 copy-start
  0.0 0.7 copy-done
  0.7 114.2 %tournament.1 = f32[4096,128]{1,0:T(8,128)S(1)} custom-call(f32[4096,128]{1,0:T(8,128)} %matrix_ref.1, s32[2,32]{1,0:T(2,128)S(1)} %copy-done), custom_call_target="tpu_custom_call" | custom-call | tf_op jit(solution)/shard_map/tournament/pallas_call | solution.py:340
  114.9 1.3 %copy.4 = f32[4096,128]{1,0:T(8,128)} copy(f32[4096,128]{1,0:T(8,128)S(1)} %tournament.1) | data formatting | bytes 4194304
Async XLA Ops:
  0.0 0.7 copy-start

commit v4 on v3

--- a/solution.py
+++ b/solution.py
@@ -11,6 +11,7 @@
 MESH = pl.DeviceIdType.MESH
 CHUNK = 256
 TILE = 8
+AHEAD = 4
 
 
 def lane_spread(value, lane):
@@ -98,8 +99,8 @@
 
 def kernel(
     total_rows, col_count, matrix_ref, active_ref, out_ref,
-    first, second, sending, result, relay, gram, norms, partial, arrived, summed, shared, rotor_parts, flags,
-    flag_sem, own_sem, a_send, a_recv, b_send, b_recv, g_send, g_recv, c_send, c_recv, local_sem,
+    first, raw, second, sending, result, relay, gram, norms, partial, arrived, summed, shared, rotor_parts, raw_parts, rotor_out, rotor_in, flags,
+    flag_sem, own_sem, a_send, a_recv, r_send, r_recv, h_send, h_recv, b_send, b_recv, g_send, g_recv, c_send, c_recv, local_sem,
 ):
     col, row = lax.axis_index("col"), lax.axis_index("row")
     odd, core = lax.rem(col, 2), lax.rem(row, 2)
@@ -139,6 +140,27 @@
             device_id_type=MESH,
         )
 
+    def r_copy(side, chunk):
+        source = (matrix_ref.at[rows_of(half, chunk)], first.at[1 - odd, rows_of(0, chunk)])[side]
+        return pltpu.make_async_remote_copy(
+            src_ref=source,
+            dst_ref=raw.at[(odd, 1 - odd)[side], rows_of(0, chunk)],
+            send_sem=r_send.at[side, chunk],
+            recv_sem=r_recv.at[side, chunk],
+            device_id=b_target,
+            device_id_type=MESH,
+        )
+
+    def h_copy():
+        return pltpu.make_async_remote_copy(
+            src_ref=rotor_out,
+            dst_ref=rotor_in,
+            send_sem=h_send,
+            recv_sem=h_recv,
+            device_id=b_target,
+            device_id_type=MESH,
+        )
+
     def b_copy(chunk):
         return pltpu.make_async_remote_copy(
             src_ref=sending.at[rows_of(0, chunk)],
@@ -193,13 +215,14 @@
             device_id_type=MESH,
         )
 
-    def each_chunk(body):
-        lax.fori_loop(0, chunks, lambda chunk, carry: (body(chunk), carry)[1], 0)
+    def each_chunk(body, low=0, high=chunks):
+        lax.fori_loop(low, high, lambda chunk, carry: (body(chunk), carry)[1], 0)
 
     own = pltpu.make_async_copy(
         matrix_ref.at[pl.ds(pl.multiple_of(half * half_rows, CHUNK), half_rows)], first.at[odd], own_sem
     )
-    each_chunk(lambda chunk: a_copy(chunk).start())
+    each_chunk(lambda chunk: (a_copy(chunk).start(), r_copy(0, chunk).start()), 0, AHEAD)
+    each_chunk(lambda chunk: a_copy(chunk).start(), AHEAD)
     own.start()
     flag_copy = pltpu.make_async_copy(active_ref, flags, flag_sem)
     flag_copy.start()
@@ -245,17 +268,20 @@
         flag = flags[step, pair].astype(jnp.float32)
         cross = jnp.concatenate([shared[step, 0, :middle], shared[step, 1, :middle]], axis=0)
         rotor = rotor_of(cross, shared[step, 0, middle:], shared[step, 1, middle:], flag, total_rows)
-        high, low = split(rotor)
-        rotor_parts[: 2 * width] = high
-        rotor_parts[2 * width : 4 * width] = high
-        rotor_parts[4 * width :] = low
-
-    def turned(held, chunk):
-        paired = jnp.concatenate([held[0, rows_of(0, chunk)], held[1, rows_of(0, chunk)]], axis=1)
-        high, low = split(paired)
-        return jnp.dot(
-            jnp.concatenate([high, low, high], axis=1), rotor_parts[...], preferred_element_type=jnp.float32
-        )
+        return rotor
+
+    def stack(parts, value):
+        high, low = split(value)
+        parts[: 2 * width] = high
+        parts[2 * width : 4 * width] = high
+        parts[4 * width :] = low
+
+    def paired(held, chunk):
+        high, low = split(jnp.concatenate([held[0, rows_of(0, chunk)], held[1, rows_of(0, chunk)]], axis=1))
+        return jnp.concatenate([high, low, high], axis=1)
+
+    def turned(held, chunk, parts):
+        return jnp.dot(paired(held, chunk), parts, preferred_element_type=jnp.float32)
 
     clear()
     own.wait()
@@ -265,27 +291,49 @@
         a_copy(chunk).wait_recv()
         add_gram(first, chunk)
 
-    each_chunk(gather_first)
-    make_rotor(0)
+    def gather_and_pass(chunk):
+        a_copy(chunk).wait_recv()
+        r_copy(1, chunk).start()
+        add_gram(first, chunk)
+
+    each_chunk(gather_and_pass, 0, AHEAD)
+    each_chunk(gather_first, AHEAD)
+    rotor = make_rotor(0)
+    rotor_out[...] = rotor[:, width:]
+    h_copy().start()
+    stack(rotor_parts, rotor)
 
     def turn_first(chunk):
-        value = turned(first, chunk)
+        value = turned(first, chunk, rotor_parts[...])
         sending[rows_of(0, chunk)] = value[:, width:]
         b_copy(chunk).start()
         second[1, rows_of(0, chunk)] = value[:, :width]
 
-    each_chunk(turn_first)
+    def turn_upper(chunk):
+        second[1, rows_of(0, chunk)] = turned(first, chunk, rotor_parts[:, :width])
+
+    each_chunk(turn_first, AHEAD)
+    each_chunk(turn_upper, 0, AHEAD)
     clear()
+    h_copy().wait_recv()
+    stack(raw_parts, rotor_in[...])
+
+    def turn_raw(chunk):
+        r_copy(0, chunk).wait_recv()
+        r_copy(1, chunk).wait_recv()
+        second[0, rows_of(0, chunk)] = turned(raw, chunk, raw_parts[...])
+        add_gram(second, chunk)
 
     def gather_second(chunk):
         b_copy(chunk).wait_recv()
         add_gram(second, chunk)
 
-    each_chunk(gather_second)
-    make_rotor(1)
+    each_chunk(turn_raw, 0, AHEAD)
+    each_chunk(gather_second, AHEAD)
+    stack(rotor_parts, make_rotor(1))
 
     def turn_second(chunk):
-        value = turned(second, chunk)
+        value = turned(second, chunk, rotor_parts[...])
         result[1, rows_of(0, chunk)] = value[:, width:]
         result[0, rows_of(0, chunk)] = value[:, :width]
 
@@ -311,7 +359,6 @@
 
     def finish(chunk):
         a_copy(chunk).wait_send()
-        b_copy(chunk).wait_send()
         c_lower(chunk).wait_send()
         c_upper(chunk).wait_send()
         c_upper(chunk).wait_recv()
@@ -325,6 +372,9 @@
             c_local(chunk).wait()
 
     each_chunk(finish)
+    each_chunk(lambda chunk: (r_copy(0, chunk).wait_send(), r_copy(1, chunk).wait_send()), 0, AHEAD)
+    each_chunk(lambda chunk: b_copy(chunk).wait_send(), AHEAD)
+    h_copy().wait_send()
 
 
 def solution(mesh):
@@ -344,6 +394,7 @@
             out_specs=pl.BlockSpec(memory_space=pl.ANY),
             scratch_shapes=[
                 pltpu.VMEM((2, half_rows, width), jnp.float32),
+                pltpu.VMEM((2, AHEAD * CHUNK, width), jnp.float32),
                 pltpu.VMEM((2, half_rows, width), jnp.float32),
                 pltpu.VMEM((half_rows, width), jnp.float32),
                 pltpu.VMEM((2, half_rows, width), jnp.float32),
@@ -355,11 +406,18 @@
                 pltpu.VMEM((2, payload, width), jnp.float32),
                 pltpu.VMEM((2, 2, payload, width), jnp.float32),
                 pltpu.VMEM((6 * width, 2 * width), jnp.bfloat16),
+                pltpu.VMEM((6 * width, width), jnp.bfloat16),
+                pltpu.VMEM((2 * width, width), jnp.float32),
+                pltpu.VMEM((2 * width, width), jnp.float32),
                 pltpu.SMEM(active.shape, jnp.int32),
                 dma(()),
                 dma(()),
                 dma((chunks,)),
                 dma((chunks,)),
+                dma((2, AHEAD)),
+                dma((2, AHEAD)),
+                dma(()),
+                dma(()),
                 dma((chunks,)),
                 dma((chunks,)),
                 dma((2, 5)),

time: 116 us -> 108 us (0.931)
  Pallas kernels: 114 us -> 106 us
    pallas_call x1, Pallas kernels: 114 us -> 106 us  [on_device(): pl.pallas_call(functools.partial(kernel, total_rows, col_count), out_shap...]
where the time goes in v4:
time: 108 us
  Pallas kernels  106 us (98%)
  local copies, waits for them, and re-layouts  2 us (2%)
    pallas_call x1, Pallas kernels, on_device(): pl.pallas_call(functools.partial(kernel, total_rows, col_count), out_shap...  106 us

profile of v4, /device:TPU:1, one launch (start us, length us, event | category | flops | bytes accessed | tf_op | source)
XLA Modules:
  0.0 107.6 jit_solution(17173414030763311514)
XLA Ops:
  0.0 0.0 copy-start
  0.0 0.7 copy-done
  0.7 105.6 %tournament.1 = f32[4096,128]{1,0:T(8,128)S(1)} custom-call(f32[4096,128]{1,0:T(8,128)} %matrix_ref.1, s32[2,32]{1,0:T(2,128)S(1)} %copy-done), custom_call_target="tpu_custom_call" | custom-call | tf_op jit(solution)/shard_map/tournament/pallas_call | solution.py:390
  106.2 1.3 %copy.4 = f32[4096,128]{1,0:T(8,128)} copy(f32[4096,128]{1,0:T(8,128)S(1)} %tournament.1) | data formatting | bytes 4194304
Async XLA Ops:
  0.0 0.7 copy-start

commit v5 on v4

--- a/solution.py
+++ b/solution.py
@@ -11,7 +11,11 @@
 MESH = pl.DeviceIdType.MESH
 CHUNK = 256
 TILE = 8
-AHEAD = 4
+AHEAD = 6
+SHORT = 5
+PIECE = 256
+WINDOW = 3
+FLIGHT = 4
 
 
 def lane_spread(value, lane):
@@ -47,9 +51,12 @@
     for other in range(len(tiles)):
         if other != block:
             value = jnp.where(inside, 0.0, tiles[other])
-            for i in range(size):
-                value = value - lane_spread(tiles[other], first + i) * rows[i]
-            result[other] = value
+            spread = [lane_spread(tiles[other], first + i) for i in range(size)]
+            upper = value - spread[7] * rows[7] - spread[6] * rows[6]
+            lower = spread[5] * rows[5] + spread[4] * rows[4]
+            early = spread[3] * rows[3] + spread[2] * rows[2]
+            late = spread[1] * rows[1] + spread[0] * rows[0]
+            result[other] = (upper - lower) - (early + late)
     solved = rows[0]
     for i in range(1, size):
         solved = jnp.where(row == i, rows[i], solved)
@@ -127,6 +134,9 @@
         pl.semaphore_signal(barrier, inc=1, device_id=device, device_id_type=MESH)
     pl.semaphore_wait(barrier, 6)
 
+    ahead_out = AHEAD - (AHEAD - SHORT) * parity
+    ahead_in = SHORT + (AHEAD - SHORT) * parity
+
     def rows_of(which, chunk):
         return pl.ds(pl.multiple_of(which * half_rows + chunk * CHUNK, CHUNK), CHUNK)
 
@@ -171,38 +181,41 @@
             device_id_type=MESH,
         )
 
-    def to_output(source, send, recv, chunk, device):
-        return pltpu.make_async_remote_copy(
-            src_ref=source.at[rows_of(0, chunk)],
-            dst_ref=out_ref.at[rows_of(half, chunk)],
-            send_sem=send.at[chunk],
-            recv_sem=recv.at[chunk],
+    def piece_of(which, piece):
+        return pl.ds(pl.multiple_of(which * half_rows + piece * PIECE, PIECE), PIECE)
+
+    def to_output(source, send, recv, piece, device):
+        return pltpu.make_async_remote_copy(
+            src_ref=source.at[piece_of(0, piece)],
+            dst_ref=out_ref.at[piece_of(half, piece)],
+            send_sem=send.at[piece],
+            recv_sem=recv.at[piece],
             device_id=device,
             device_id_type=MESH,
         )
 
-    def c_upper(chunk):
-        return to_output(result.at[0], c_send.at[0], c_recv.at[0], chunk, partner)
-
-    def c_lower(chunk):
-        return to_output(result.at[1], c_send.at[1], c_recv.at[1], chunk, b_target)
-
-    def c_passed(chunk):
-        return to_output(relay, c_send.at[0], c_recv.at[0], chunk, partner)
-
-    def c_relay(chunk):
-        return pltpu.make_async_remote_copy(
-            src_ref=result.at[1, rows_of(0, chunk)],
-            dst_ref=relay.at[rows_of(0, chunk)],
-            send_sem=c_send.at[1, chunk],
-            recv_sem=c_recv.at[1, chunk],
+    def c_upper(piece):
+        return to_output(result.at[0], c_send.at[0], c_recv.at[0], piece, partner)
+
+    def c_lower(piece):
+        return to_output(result.at[1], c_send.at[1], c_recv.at[1], piece, b_target)
+
+    def c_passed(piece):
+        return to_output(relay, c_send.at[0], c_recv.at[0], piece, partner)
+
+    def c_relay(piece):
+        return pltpu.make_async_remote_copy(
+            src_ref=result.at[1, piece_of(0, piece)],
+            dst_ref=relay.at[piece_of(0, piece)],
+            send_sem=c_send.at[1, piece],
+            recv_sem=c_recv.at[1, piece],
             device_id=b_target,
             device_id_type=MESH,
         )
 
-    def c_local(chunk):
+    def c_local(piece):
         return pltpu.make_async_copy(
-            result.at[0, rows_of(0, chunk)], out_ref.at[rows_of(half, chunk)], local_sem.at[chunk]
+            result.at[0, piece_of(0, piece)], out_ref.at[piece_of(half, piece)], local_sem.at[piece]
         )
 
     def g_copy(source, target, step, stage, device):
@@ -221,8 +234,7 @@
     own = pltpu.make_async_copy(
         matrix_ref.at[pl.ds(pl.multiple_of(half * half_rows, CHUNK), half_rows)], first.at[odd], own_sem
     )
-    each_chunk(lambda chunk: (a_copy(chunk).start(), r_copy(0, chunk).start()), 0, AHEAD)
-    each_chunk(lambda chunk: a_copy(chunk).start(), AHEAD)
+    each_chunk(lambda chunk: (a_copy(chunk).start(), r_copy(0, chunk).start()), 0, WINDOW)
     own.start()
     flag_copy = pltpu.make_async_copy(active_ref, flags, flag_sem)
     flag_copy.start()
@@ -243,7 +255,7 @@
         norms[0] += jnp.sum((upper * upper).reshape(CHUNK // 8, 8, width), axis=0)
         norms[1] += jnp.sum((lower * lower).reshape(CHUNK // 8, 8, width), axis=0)
 
-    def make_rotor(step):
+    def share_gram(step):
         middle = width // 2
         cross = (gram[:width, :width] + gram[width:, width:]) + (gram[:width, width:] + gram[width:, :width])
         for part in range(2):
@@ -265,6 +277,8 @@
         copy = g_copy(shared.at[step, core], shared.at[step, core], step, 4, sibling)
         copy.start()
         copy.wait()
+    def make_rotor(step):
+        middle = width // 2
         flag = flags[step, pair].astype(jnp.float32)
         cross = jnp.concatenate([shared[step, 0, :middle], shared[step, 1, :middle]], axis=0)
         rotor = rotor_of(cross, shared[step, 0, middle:], shared[step, 1, middle:], flag, total_rows)
@@ -289,15 +303,25 @@
 
     def gather_first(chunk):
         a_copy(chunk).wait_recv()
+        even, place = lax.rem(chunk, 2) == 0, chunk // 2
+
+        @pl.when(even)
+        def _():
+            r_copy(1, place).start()
+
+        @pl.when(jnp.logical_not(even) & (place + WINDOW < ahead_out))
+        def _():
+            r_copy(0, place + WINDOW).start()
+
+        @pl.when(chunk + WINDOW < chunks)
+        def _():
+            a_copy(chunk + WINDOW).start()
+
         add_gram(first, chunk)
 
-    def gather_and_pass(chunk):
-        a_copy(chunk).wait_recv()
-        r_copy(1, chunk).start()
-        add_gram(first, chunk)
-
-    each_chunk(gather_and_pass, 0, AHEAD)
-    each_chunk(gather_first, AHEAD)
+    each_chunk(gather_first)
+    each_chunk(lambda chunk: r_copy(1, chunk).start(), chunks // 2, ahead_out)
+    share_gram(0)
     rotor = make_rotor(0)
     rotor_out[...] = rotor[:, width:]
     h_copy().start()
@@ -306,15 +330,15 @@
     def turn_first(chunk):
         value = turned(first, chunk, rotor_parts[...])
         sending[rows_of(0, chunk)] = value[:, width:]
-        b_copy(chunk).start()
         second[1, rows_of(0, chunk)] = value[:, :width]
 
     def turn_upper(chunk):
         second[1, rows_of(0, chunk)] = turned(first, chunk, rotor_parts[:, :width])
 
-    each_chunk(turn_first, AHEAD)
-    each_chunk(turn_upper, 0, AHEAD)
+    each_chunk(turn_first, ahead_out)
+    each_chunk(turn_upper, 0, ahead_out)
     clear()
+    each_chunk(lambda chunk: b_copy(chunk).start(), ahead_out)
     h_copy().wait_recv()
     stack(raw_parts, rotor_in[...])
 
@@ -328,53 +352,73 @@
         b_copy(chunk).wait_recv()
         add_gram(second, chunk)
 
-    each_chunk(turn_raw, 0, AHEAD)
-    each_chunk(gather_second, AHEAD)
+    each_chunk(turn_raw, 0, ahead_in)
+    each_chunk(gather_second, ahead_in)
+    share_gram(1)
     stack(rotor_parts, make_rotor(1))
 
     def turn_second(chunk):
         value = turned(second, chunk, rotor_parts[...])
         result[1, rows_of(0, chunk)] = value[:, width:]
         result[0, rows_of(0, chunk)] = value[:, :width]
-
+        low, high = chunk * (CHUNK // PIECE), (chunk + 1) * (CHUNK // PIECE)
+
+        @pl.when(high <= FLIGHT)
+        def _():
+            each_chunk(begin, low, high)
+
+        @pl.when(odd == 1)
+        def _():
+            each_chunk(lambda piece: c_local(piece).start(), low, high)
+
+    def begin(piece):
         @pl.when(odd == 0)
         def _():
-            c_relay(chunk).start()
-            c_upper(chunk).start()
+            c_relay(piece).start()
+            c_upper(piece).start()
 
         @pl.when(odd == 1)
         def _():
-            c_lower(chunk).start()
-            c_local(chunk).start()
+            c_lower(piece).start()
 
     each_chunk(turn_second)
-
-    @pl.when(odd == 1)
-    def _():
-        def pass_on(chunk):
-            c_relay(chunk).wait_recv()
-            c_passed(chunk).start()
-
-        each_chunk(pass_on)
-
-    def finish(chunk):
-        a_copy(chunk).wait_send()
-        c_lower(chunk).wait_send()
-        c_upper(chunk).wait_send()
-        c_upper(chunk).wait_recv()
-
+    pieces = half_rows // PIECE
+
+    def pace(piece):
         @pl.when(odd == 0)
         def _():
-            c_lower(chunk).wait_recv()
+            c_upper(piece).wait_send()
 
         @pl.when(odd == 1)
         def _():
-            c_local(chunk).wait()
-
-    each_chunk(finish)
-    each_chunk(lambda chunk: (r_copy(0, chunk).wait_send(), r_copy(1, chunk).wait_send()), 0, AHEAD)
-    each_chunk(lambda chunk: b_copy(chunk).wait_send(), AHEAD)
+            c_relay(piece).wait_recv()
+            c_passed(piece).start()
+
+        c_lower(piece).wait_send()
+
+        @pl.when(piece + FLIGHT < pieces)
+        def _():
+            begin(piece + FLIGHT)
+
+    each_chunk(pace, 0, pieces)
+
+    def finish(piece):
+        c_upper(piece).wait_recv()
+
+        @pl.when(odd == 0)
+        def _():
+            c_lower(piece).wait_recv()
+
+        @pl.when(odd == 1)
+        def _():
+            c_passed(piece).wait_send()
+            c_local(piece).wait()
+
+    each_chunk(finish, 0, pieces)
     h_copy().wait_send()
+    each_chunk(lambda chunk: b_copy(chunk).wait_send(), ahead_out)
+    each_chunk(lambda chunk: (r_copy(0, chunk).wait_send(), r_copy(1, chunk).wait_send()), 0, ahead_out)
+    each_chunk(lambda chunk: a_copy(chunk).wait_send())
 
 
 def solution(mesh):
@@ -422,9 +466,9 @@
                 dma((chunks,)),
                 dma((2, 5)),
                 dma((2, 5)),
-                dma((2, chunks)),
-                dma((2, chunks)),
-                dma((chunks,)),
+                dma((2, half_rows // PIECE)),
+                dma((2, half_rows // PIECE)),
+                dma((half_rows // PIECE,)),
             ],
             compiler_params=pltpu.CompilerParams(
                 collective_id=0, has_side_effects=True, vmem_limit_bytes=50 * 2**20

time: 108 us -> 105 us (0.972)
  Pallas kernels: 106 us -> 103 us
    pallas_call x1, Pallas kernels: 106 us -> 103 us  [on_device(): pl.pallas_call(functools.partial(kernel, total_rows, col_count), out_shap...]
where the time goes in v5:
time: 105 us
  Pallas kernels  103 us (98%)
  local copies, waits for them, and re-layouts  2 us (2%)
    pallas_call x1, Pallas kernels, on_device(): pl.pallas_call(functools.partial(kernel, total_rows, col_count), out_shap...  103 us

profile of v5, /device:TPU:1, one launch (start us, length us, event | category | flops | bytes accessed | tf_op | source)
XLA Modules:
  0.0 105.3 jit_solution(9286125674650278337)
XLA Ops:
  0.0 0.0 copy-start
  0.0 0.7 copy-done
  0.7 103.3 %tournament.1 = f32[4096,128]{1,0:T(8,128)S(1)} custom-call(f32[4096,128]{1,0:T(8,128)} %matrix_ref.1, s32[2,32]{1,0:T(2,128)S(1)} %copy-done), custom_call_target="tpu_custom_call" | custom-call | tf_op jit(solution)/shard_map/tournament/pallas_call | solution.py:434
  104.0 1.3 %copy.4 = f32[4096,128]{1,0:T(8,128)} copy(f32[4096,128]{1,0:T(8,128)S(1)} %tournament.1) | data formatting | bytes 4194304
Async XLA Ops:
  0.0 0.7 copy-start

commit v6 on v5

--- a/solution.py
+++ b/solution.py
@@ -11,7 +11,7 @@
 MESH = pl.DeviceIdType.MESH
 CHUNK = 256
 TILE = 8
-AHEAD = 6
+AHEAD = 7
 SHORT = 5
 PIECE = 256
 WINDOW = 3
@@ -137,8 +137,8 @@
     ahead_out = AHEAD - (AHEAD - SHORT) * parity
     ahead_in = SHORT + (AHEAD - SHORT) * parity
 
-    def rows_of(which, chunk):
-        return pl.ds(pl.multiple_of(which * half_rows + chunk * CHUNK, CHUNK), CHUNK)
+    def rows_of(which, chunk, count=1):
+        return pl.ds(pl.multiple_of(which * half_rows + chunk * CHUNK, CHUNK), count * CHUNK)
 
     def a_copy(chunk):
         return pltpu.make_async_remote_copy(
@@ -243,17 +243,17 @@
         gram[...] = jnp.zeros_like(gram)
         norms[...] = jnp.zeros_like(norms)
 
-    def add_gram(held, chunk):
-        upper = held[0, rows_of(0, chunk)]
-        lower = held[1, rows_of(0, chunk)]
+    def add_gram(held, chunk, count=1):
+        upper = held[0, rows_of(0, chunk, count)]
+        lower = held[1, rows_of(0, chunk, count)]
         gram[...] += lax.dot_general(
             jnp.concatenate(split(upper), axis=1),
             jnp.concatenate(split(lower), axis=1),
             (((0,), (0,)), ((), ())),
             preferred_element_type=jnp.float32,
         )
-        norms[0] += jnp.sum((upper * upper).reshape(CHUNK // 8, 8, width), axis=0)
-        norms[1] += jnp.sum((lower * lower).reshape(CHUNK // 8, 8, width), axis=0)
+        norms[0] += jnp.sum((upper * upper).reshape(count * CHUNK // 8, 8, width), axis=0)
+        norms[1] += jnp.sum((lower * lower).reshape(count * CHUNK // 8, 8, width), axis=0)
 
     def share_gram(step):
         middle = width // 2
@@ -290,12 +290,12 @@
         parts[2 * width : 4 * width] = high
         parts[4 * width :] = low
 
-    def paired(held, chunk):
-        high, low = split(jnp.concatenate([held[0, rows_of(0, chunk)], held[1, rows_of(0, chunk)]], axis=1))
+    def paired(held, chunk, count):
+        high, low = split(jnp.concatenate([held[0, rows_of(0, chunk, count)], held[1, rows_of(0, chunk, count)]], axis=1))
         return jnp.concatenate([high, low, high], axis=1)
 
-    def turned(held, chunk, parts):
-        return jnp.dot(paired(held, chunk), parts, preferred_element_type=jnp.float32)
+    def turned(held, chunk, parts, count=1):
+        return jnp.dot(paired(held, chunk, count), parts, preferred_element_type=jnp.float32)
 
     clear()
     own.wait()
@@ -342,17 +342,19 @@
     h_copy().wait_recv()
     stack(raw_parts, rotor_in[...])
 
-    def turn_raw(chunk):
-        r_copy(0, chunk).wait_recv()
-        r_copy(1, chunk).wait_recv()
-        second[0, rows_of(0, chunk)] = turned(raw, chunk, raw_parts[...])
-        add_gram(second, chunk)
+    def turn_raw(chunk, count=1):
+        for place in range(count):
+            r_copy(0, chunk + place).wait_recv()
+            r_copy(1, chunk + place).wait_recv()
+        second[0, rows_of(0, chunk, count)] = turned(raw, chunk, raw_parts[...], count)
+        add_gram(second, chunk, count)
 
     def gather_second(chunk):
         b_copy(chunk).wait_recv()
         add_gram(second, chunk)
 
-    each_chunk(turn_raw, 0, ahead_in)
+    each_chunk(lambda double: turn_raw(2 * double, 2), 0, ahead_in // 2)
+    each_chunk(turn_raw, ahead_in // 2 * 2, ahead_in)
     each_chunk(gather_second, ahead_in)
     share_gram(1)
     stack(rotor_parts, make_rotor(1))

time: 105 us -> 104 us (level)
    pallas_call x1, Pallas kernels: 103 us -> 102 us  [on_device(): pl.pallas_call(functools.partial(kernel, total_rows, col_count), out_shap...]
where the time goes in v6:
time: 104 us
  Pallas kernels  102 us (98%)
  local copies, waits for them, and re-layouts  2 us (2%)
    pallas_call x1, Pallas kernels, on_device(): pl.pallas_call(functools.partial(kernel, total_rows, col_count), out_shap...  102 us

profile of v6, /device:TPU:1, one launch (start us, length us, event | category | flops | bytes accessed | tf_op | source)
XLA Modules:
  0.0 103.6 jit_solution(1517741029355526785)
XLA Ops:
  0.0 0.0 copy-start
  0.0 0.7 copy-done
  0.7 101.6 %tournament.1 = f32[4096,128]{1,0:T(8,128)S(1)} custom-call(f32[4096,128]{1,0:T(8,128)} %matrix_ref.1, s32[2,32]{1,0:T(2,128)S(1)} %copy-done), custom_call_target="tpu_custom_call" | custom-call | tf_op jit(solution)/shard_map/tournament/pallas_call | solution.py:436
  102.3 1.3 %copy.4 = f32[4096,128]{1,0:T(8,128)} copy(f32[4096,128]{1,0:T(8,128)S(1)} %tournament.1) | data formatting | bytes 4194304
Async XLA Ops:
  0.0 0.7 copy-start

commit v7 on v6

--- a/solution.py
+++ b/solution.py
@@ -332,11 +332,12 @@
         sending[rows_of(0, chunk)] = value[:, width:]
         second[1, rows_of(0, chunk)] = value[:, :width]
 
-    def turn_upper(chunk):
-        second[1, rows_of(0, chunk)] = turned(first, chunk, rotor_parts[:, :width])
+    def turn_upper(chunk, count=1):
+        second[1, rows_of(0, chunk, count)] = turned(first, chunk, rotor_parts[:, :width], count)
 
     each_chunk(turn_first, ahead_out)
-    each_chunk(turn_upper, 0, ahead_out)
+    each_chunk(lambda double: turn_upper(2 * double, 2), 0, ahead_out // 2)
+    each_chunk(turn_upper, ahead_out // 2 * 2, ahead_out)
     clear()
     each_chunk(lambda chunk: b_copy(chunk).start(), ahead_out)
     h_copy().wait_recv()

time: 104 us -> 104 us (level)
  no operation moved by 1% of the time
where the time goes in v7:
time: 104 us
  Pallas kernels  102 us (98%)
  local copies, waits for them, and re-layouts  2 us (2%)
    pallas_call x1, Pallas kernels, on_device(): pl.pallas_call(functools.partial(kernel, total_rows, col_count), out_shap...  102 us

profile of v7, /device:TPU:1, one launch (start us, length us, event | category | flops | bytes accessed | tf_op | source)
XLA Modules:
  0.0 103.6 jit_solution(17742946931179747826)
XLA Ops:
  0.0 0.0 copy-start
  0.0 0.7 copy-done
  0.7 101.6 %tournament.1 = f32[4096,128]{1,0:T(8,128)S(1)} custom-call(f32[4096,128]{1,0:T(8,128)} %matrix_ref.1, s32[2,32]{1,0:T(2,128)S(1)} %copy-done), custom_call_target="tpu_custom_call" | custom-call | tf_op jit(solution)/shard_map/tournament/pallas_call | solution.py:437
  102.3 1.3 %copy.4 = f32[4096,128]{1,0:T(8,128)} copy(f32[4096,128]{1,0:T(8,128)S(1)} %tournament.1) | data formatting | bytes 4194304
Async XLA Ops:
  0.0 0.7 copy-start
